TPU v7x, 32 devices: a whole 2x2x4 slice. The times are simulated.
32 devices in a mesh: wide: 8 (over y, x, core), blk: 4 (over z).
Axes of the slice: x: 2, y: 2, z: 4, core: 2. Of those that a mesh axis runs over, the one named last changes fastest.
Arguments:
- tokens: bfloat16 [16384, 8192], P(('wide', 'blk')), may hold values from -6 to 6
- base_key_matrix: bfloat16 [8192, 1024], P('blk'), may hold values from -0.0625 to 0.0625
- adapter_down_weights: bfloat16 [256, 64, 8192], P(('wide', 'blk')), may hold values from -0.0625 to 0.0625
- adapter_up_weights: bfloat16 [256, 64, 1024], P(('wide', 'blk')), may hold values from -0.75 to 0.75
- request_adapter_index: int32 [256], P(('wide', 'blk')), may hold values from 0 to 255, as said below
Outputs:
- keys: bfloat16 [16384, 1024], P(('wide', 'blk'))
Inputs may be any that keep to these rules, and one draw needn't show every extreme that they name: `request_adapter_index`: request r lies on device r // 8 of wide+blk; adapter a lies on device a // 8. Each request's adapter lies on a device with the same blk index as the request. Of one device's requests at most 2 have adapters on any one wide index; for every blk index one wide index holds the adapters of exactly 2 requests of every device with that blk index.
All inputs are finite; a program needn't handle non-finite values.
Results may differ from a plain program's by a relative error of at most 0.005.
Values may be sent and summed in bfloat16 or wider, within the bound.
A program may use at most 192 MiB of HBM per device.

v0:
```python
import jax
import jax.numpy as jnp
from jax import lax
from jax.sharding import PartitionSpec as P

SEQ = 64
CAP = 2


def per_device(
    tokens, base_key_matrix, adapter_down_weights, adapter_up_weights, request_adapter_index
):
    wide_count = lax.axis_size("wide")
    block_count = lax.axis_size("blk")
    resident_count = adapter_down_weights.shape[0]
    req_count = request_adapter_index.shape[0]
    width = tokens.shape[1]
    out_width = base_key_matrix.shape[1]
    slot_count = wide_count * CAP
    base = jnp.dot(
        tokens,
        lax.all_gather(base_key_matrix, "blk", axis=0, tiled=True),
        preferred_element_type=jnp.float32,
    )
    owner_wide = request_adapter_index // (resident_count * block_count)
    local_ids = request_adapter_index % resident_count
    positions = jnp.arange(req_count, dtype=jnp.int32)
    same_owner = owner_wide[:, None] == owner_wide[None, :]
    earlier = positions[None, :] < positions[:, None]
    rank = jnp.sum(jnp.where(same_owner & earlier, 1, 0), axis=1).astype(jnp.int32)
    slot_of_req = owner_wide * CAP + rank
    member = slot_of_req[:, None] == jnp.arange(slot_count, dtype=jnp.int32)[None, :]
    valid = jnp.any(member, axis=0)
    source_req = jnp.sum(jnp.where(member, positions[:, None], 0), axis=0)
    slot_local = jnp.where(valid, jnp.take(local_ids, source_req, axis=0), 0)[:, None]
    requests = tokens.reshape(req_count, SEQ, width)
    outgoing = jnp.take(requests, source_req, axis=0)
    arrived, received_adapter_index = (
        lax.all_to_all(outgoing, "wide", split_axis=0, concat_axis=0, tiled=True),
        lax.all_to_all(slot_local, "wide", split_axis=0, concat_axis=0, tiled=True),
    )
    selected_down_weight = jnp.take(adapter_down_weights, received_adapter_index[:, 0], axis=0)
    selected_up_weight = jnp.take(adapter_up_weights, received_adapter_index[:, 0], axis=0)
    shrink = jnp.einsum(
        "sqd,srd->sqr", arrived, selected_down_weight, preferred_element_type=jnp.float32
    ).astype(jnp.bfloat16)
    expand = jnp.einsum(
        "sqr,srk->sqk", shrink, selected_up_weight, preferred_element_type=jnp.float32
    ).astype(jnp.bfloat16)
    returned = lax.all_to_all(expand, "wide", split_axis=0, concat_axis=0, tiled=True)
    delta = jnp.take(returned, slot_of_req, axis=0)
    keys = (base + delta.reshape(tokens.shape[0], out_width).astype(jnp.float32)).astype(
        jnp.bfloat16
    )
    return keys


def solution(mesh):
    return jax.shard_map(
        per_device,
        mesh=mesh,
        in_specs=(
            P(("wide", "blk"), None),
            P("blk", None),
            P(("wide", "blk"), None, None),
            P(("wide", "blk"), None, None),
            P(("wide", "blk")),
        ),
        out_specs=P(("wide", "blk"), None),
        check_vma=False,
    )
```

profile of v0, /device:TPU:0, one launch (start us, length us, event | category | flops | bytes accessed | tf_op | source)
XLA Modules:
  0.0 320.9 jit_solution(11483564231436792549)
XLA Ops:
  6.5 0.7 all-gather.2.cloned.1.call-update
  7.3 0.7 and_select_fusion
  7.9 0.2 select_reduce_fusion.1
  8.1 0.1 fusion.16
  8.2 0.1 reduce_or.12
  8.5 0.7 gather_fusion
  9.2 0.6 select_select_fusion
  9.8 5.2 %all-to-all-start.1 = ((s32[8,2,1]{1,2,0:T(1,128)}), s32[8,2,1]{1,2,0:T(1,128)S(1)}, u32[]{:S(2)}, u32[]{:S(2)}) async-start(s32[8,2,1]{1,2,0:T(1,128)} %bitcast.3), calls=%async_computation.1 | async-start | bytes 8192 | tf_op jit(solution)/shard_map/all_to_all | solution.py:40
  15.0 12.3 %gather_fusion.3 = bf16[16,64,8192]{2,1,0:T(8,128)(2,1)} fusion(bf16[8,64,8192]{2,1,0:T(8,128)(2,1)} %bitcast.15, s32[1024]{0:T(1024)S(1)} %pad_clamp_fusion.4), kind=kCustom, calls=%fused_computation.clone | custom fusion | bytes 33554496 | tf_op jit(solution)/shard_map/jit(_take)/gather | solution.py:37
  27.4 14.5 %broadcast_select_fusion = bf16[16,64,8192]{2,1,0:T(8,128)(2,1)} fusion(bf16[16,64,8192]{2,1,0:T(8,128)(2,1)} %gather_fusion.3, pred[16]{0:T(512)(128)(4,1)S(1)} %compare_and_fusion.1), kind=kLoop, calls=%fused_computation.8 | loop fusion | flops 8388608 | bytes 33554448 | tf_op jit(solution)/shard_map/jit(_take)/select_n | solution.py:37
  41.9 5.8 %all-to-all-start = ((bf16[16,64,8192]{2,1,0:T(8,128)(2,1)}), bf16[16,64,8192]{2,1,0:T(8,128)(2,1)}, u32[]{:S(2)}, u32[]{:S(2)}) async-start(bf16[16,64,8192]{2,1,0:T(8,128)(2,1)} %broadcast_select_fusion), calls=%async_computation | async-start | bytes 33554432 | tf_op jit(solution)/shard_map/all_to_all | solution.py:39
  47.7 0.5 broadcast.225
  48.2 0.7 reduce.5
  49.0 0.7 gather_fusion.1
  49.7 10.4 %gather_fusion.4 = bf16[16,64,8192]{2,1,0:T(8,128)(2,1)} fusion(bf16[8,64,8192]{2,1,0:T(8,128)(2,1)} %param.9, s32[1024]{0:T(1024)S(1)} %pad_clamp_fusion.2), kind=kCustom, calls=%fused_computation.1.clone | custom fusion | bytes 33554496 | tf_op jit(solution)/shard_map/jit(_take)/gather | solution.py:42
  60.1 171.4 %all-to-all-done = bf16[16,64,8192]{2,1,0:T(8,128)(2,1)} async-done(((bf16[16,64,8192]{2,1,0:T(8,128)(2,1)}), bf16[16,64,8192]{2,1,0:T(8,128)(2,1)}, u32[]{:S(2)}, u32[]{:S(2)}) %all-to-all-start) | async-done | bytes 16777248 | tf_op jit(solution)/shard_map/all_to_all | solution.py:39
  231.6 14.6 %fusion.7 = bf16[16,64,1024]{2,1,0:T(8,128)(2,1)} fusion(bf16[16,64,1024]{2,1,0:T(8,128)(2,1)S(1)} %gather_fusion.1, pred[16]{0:T(512)(128)(4,1)S(1)} %compare_and_fusion, bf16[16,64,8192]{2,1,0:T(8,128)(2,1)} %all-to-all-done, bf16[16,64,8192]{2,1,0:T(8,128)(2,1)} %gather_fusion.4), kind=kOutput, calls=%fused_computation.14 | convolution fusion | flops 1218510848 | bytes 37748752 | tf_op jit(solution)/shard_map/sqr,srk->sqk/dot_general | solution.py:47
  246.2 3.6 %all-to-all-start.2 = ((bf16[16,64,1024]{2,1,0:T(8,128)(2,1)}), bf16[16,64,1024]{2,1,0:T(8,128)(2,1)S(1)}, u32[]{:S(2)}, u32[]{:S(2)}) async-start(bf16[16,64,1024]{2,1,0:T(8,128)(2,1)} %fusion.7), calls=%async_computation.2 | async-start | bytes 4194304 | tf_op jit(solution)/shard_map/all_to_all | solution.py:50
  249.8 0.1 broadcast_in_dim.70
  249.9 26.4 %all-to-all-done.2 = bf16[16,64,1024]{2,1,0:T(8,128)(2,1)S(1)} async-done(((bf16[16,64,1024]{2,1,0:T(8,128)(2,1)}), bf16[16,64,1024]{2,1,0:T(8,128)(2,1)S(1)}, u32[]{:S(2)}, u32[]{:S(2)}) %all-to-all-start.2) | async-done | bytes 2097184 | tf_op jit(solution)/shard_map/all_to_all | solution.py:50
  276.3 1.6 gather_fusion.2
  277.9 1.4 bitcast_select_fusion
  279.3 19.1 %all-gather.2.cloned.1.call-done = bf16[8192,1024]{1,0:T(8,128)(2,1)} async-done(((bf16[2048,1024]{1,0:T(8,128)(2,1)}), bf16[8192,1024]{1,0:T(8,128)(2,1)}) %all-gather.2.cloned.1.call-update) | async-done | bytes 16777232 | tf_op jit(solution)/shard_map/all_gather | solution.py:22
  298.4 15.6 %add_convert_fusion = bf16[512,1024]{1,0:T(8,128)(2,1)} fusion(bf16[512,1024]{1,0:T(8,128)(2,1)S(1)} %bitcast_select_fusion, bf16[512,8192]{1,0:T(8,128)(2,1)} %param.7, bf16[8192,1024]{1,0:T(8,128)(2,1)} %all-gather.2.cloned.1.call-done), kind=kOutput, calls=%fused_computation.10 | convolution fusion | flops 8591507456 | bytes 27262976 | tf_op jit(solution)/shard_map/dot_general | solution.py:20
  (23 shorter events, 0.6 us)
Async XLA Ops:
  6.5 42.4 %copy-start = (bf16[8,64,1024]{2,1,0:T(8,128)(2,1)S(1)}, bf16[8,64,1024]{2,1,0:T(8,128)(2,1)}, u32[]{:S(2)}) copy-start(bf16[8,64,1024]{2,1,0:T(8,128)(2,1)} %param.10) | copy-start | bytes 3145732
  6.5 291.9 %all-gather.2.cloned.1.call-start = ((), (), s32[]{:S(2)}) async-start(), calls=%async_computation.3 | async-start | bytes 20971520 | tf_op jit(solution)/shard_map/all_gather | solution.py:22
  9.8 32.0 %all-to-all-start.1 = ((s32[8,2,1]{1,2,0:T(1,128)}), s32[8,2,1]{1,2,0:T(1,128)S(1)}, u32[]{:S(2)}, u32[]{:S(2)}) async-start(s32[8,2,1]{1,2,0:T(1,128)} %bitcast.3), calls=%async_computation.1 | async-start | bytes 8192 | tf_op jit(solution)/shard_map/all_to_all | solution.py:40
  41.9 189.7 %all-to-all-start = ((bf16[16,64,8192]{2,1,0:T(8,128)(2,1)}), bf16[16,64,8192]{2,1,0:T(8,128)(2,1)}, u32[]{:S(2)}, u32[]{:S(2)}) async-start(bf16[16,64,8192]{2,1,0:T(8,128)(2,1)} %broadcast_select_fusion), calls=%async_computation | async-start | bytes 33554432 | tf_op jit(solution)/shard_map/all_to_all | solution.py:39
  246.2 30.2 %all-to-all-start.2 = ((bf16[16,64,1024]{2,1,0:T(8,128)(2,1)}), bf16[16,64,1024]{2,1,0:T(8,128)(2,1)S(1)}, u32[]{:S(2)}, u32[]{:S(2)}) async-start(bf16[16,64,1024]{2,1,0:T(8,128)(2,1)} %fusion.7), calls=%async_computation.2 | async-start | bytes 4194304 | tf_op jit(solution)/shard_map/all_to_all | solution.py:50
Sparse Core Ops, SparseCore 0:
  8.9 289.4 all-gather.1
where the time goes:
time: 321 us
  waiting for transfers between devices  218 us (68%)
  matrix products  30.2 us (9%)
  local copies, waits for them, and re-layouts  26.8 us (8%)
  other arithmetic  18.2 us (6%)
  starting transfers between devices  14.5 us (5%)
  between operations  13.5 us (4%)
    all_to_all x1, waiting for transfers between devices, per_device(): lax.all_to_all(outgoing, 'wide', split_axis=0, concat_axis=0, tiled=True)  171 us
    all_to_all x1, waiting for transfers between devices, per_device(): lax.all_to_all(expand, 'wide', split_axis=0, concat_axis=0, tiled=True)  26.4 us
    all_gather x1, waiting for transfers between devices, per_device(): lax.all_gather(base_key_matrix, 'blk', axis=0, tiled=True)  19.1 us
    dot_general x1, matrix products, per_device(): jnp.dot(tokens, lax.all_gather(base_key_matrix, 'blk', axis=0, tiled=True...  15.6 us
    dot_general x1, matrix products, per_device(): jnp.einsum('sqr,srk->sqk', shrink, selected_up_weight, preferred_element_...  14.6 us
    select_n x2, other arithmetic, per_device(): outgoing = jnp.take(requests, source_req, axis=0)  14.5 us
    gather x1, local copies, waits for them, and re-layouts, per_device(): outgoing = jnp.take(requests, source_req, axis=0)  12.3 us
    gather x1, local copies, waits for them, and re-layouts, per_device(): jnp.take(adapter_down_weights, received_adapter_index[:, 0], axis=0)  10.4 us
  transfers between devices with their start and end apart: 4, of which 3 were waited for; matrix products, arithmetic and copies ran while one was open for 19% of the time, Pallas kernels for 0%

commit v1 on v0

--- a/solution.py
+++ b/solution.py
@@ -5,6 +5,27 @@
 
 SEQ = 64
 CAP = 2
+
+
+def ring_gather(value, axis, dim):
+    size, place, rows = (lax.axis_size(axis), lax.axis_index(axis), value.shape[dim])
+    ahead = [(i, (i + 1) % size) for i in range(size)]
+    left = [(i, (i - 1) % size) for i in range(size)]
+    out = jnp.zeros((*value.shape[:dim], size * rows, *value.shape[dim + 1 :]), value.dtype)
+    out = lax.dynamic_update_slice_in_dim(out, value, place * rows, axis=dim)
+    from_left = from_right = value
+    half = size // 2
+    for turn in range(1, half + 1):
+        from_left = lax.ppermute(from_left, axis, ahead)
+        out = lax.dynamic_update_slice_in_dim(
+            out, from_left, (place - turn) % size * rows, axis=dim
+        )
+        if turn < size - half:
+            from_right = lax.ppermute(from_right, axis, left)
+            out = lax.dynamic_update_slice_in_dim(
+                out, from_right, (place + turn) % size * rows, axis=dim
+            )
+    return out
 
 
 def per_device(
@@ -18,9 +39,7 @@
     out_width = base_key_matrix.shape[1]
     slot_count = wide_count * CAP
     base = jnp.dot(
-        tokens,
-        lax.all_gather(base_key_matrix, "blk", axis=0, tiled=True),
-        preferred_element_type=jnp.float32,
+        tokens, ring_gather(base_key_matrix, "blk", 0), preferred_element_type=jnp.float32
     )
     owner_wide = request_adapter_index // (resident_count * block_count)
     local_ids = request_adapter_index % resident_count

time: 321 us -> 341 us (1.062)
  local copies, waits for them, and re-layouts: 26.8 us -> 48.5 us
  between operations: 13.5 us -> 0.17 us
  waiting for transfers between devices: 218 us -> 228 us
  starting transfers between devices: 14.5 us -> 18.6 us
    ppermute x0 -> x3, waiting for transfers between devices: none -> 145 us  [the longest x2 145 us: ring_gather(): from_left = lax.ppermute(from_left, axis, ahead)]
    all_to_all x1, waiting for transfers between devices: 171 us -> 77.9 us  [per_device(): lax.all_to_all(outgoing, 'wide', split_axis=0, concat_axis=0, tiled=True)]
    all_to_all x1, waiting for transfers between devices: 26.4 us -> 0.01 us  [per_device(): lax.all_to_all(expand, 'wide', split_axis=0, concat_axis=0, tiled=True)]
    all_gather x1 -> x0, waiting for transfers between devices: 19.1 us -> none  [per_device(): lax.all_gather(base_key_matrix, 'blk', axis=0, tiled=True)]
    dynamic_update_slice x0 -> x4, local copies, waits for them, and re-layouts: none -> 16.1 us  [the longest x2 9.14 us: ring_gather(): lax.dynamic_update_slice_in_dim(out, from_left, (place - turn) % size * r...]
    broadcast_in_dim x0 -> x1, local copies, waits for them, and re-layouts: none -> 6.63 us  [ring_gather(): jnp.zeros((*value.shape[:dim], size * rows, *value.shape[dim + 1:]), valu...]
    all_to_all x1, waiting for transfers between devices: 0.01 us -> 4.58 us  [per_device(): lax.all_to_all(slot_local, 'wide', split_axis=0, concat_axis=0, tiled=True)]
    ppermute x0 -> x3, starting transfers between devices: none -> 3.88 us  [the longest x1 2.25 us: ring_gather(): from_right = lax.ppermute(from_right, axis, left)]
  transfers between devices with their start and end apart: 4 -> 6, of which waited for: 3 -> 4; matrix products, arithmetic and copies ran while one was open for 19% -> 14% of each run, Pallas kernels for 0% -> 0%
where the time goes in v1:
time: 341 us
  waiting for transfers between devices  228 us (67%)
  local copies, waits for them, and re-layouts  48.5 us (14%)
  matrix products  29.6 us (9%)
  starting transfers between devices  18.6 us (5%)
  other arithmetic  16.6 us (5%)
    ppermute x2, waiting for transfers between devices, ring_gather(): from_left = lax.ppermute(from_left, axis, ahead)  145 us
    all_to_all x1, waiting for transfers between devices, per_device(): lax.all_to_all(outgoing, 'wide', split_axis=0, concat_axis=0, tiled=True)  77.9 us
    dot_general x1, matrix products, per_device(): jnp.dot(tokens, ring_gather(base_key_matrix, 'blk', 0), preferred_element...  15 us
    dot_general x1, matrix products, per_device(): jnp.einsum('sqr,srk->sqk', shrink, selected_up_weight, preferred_element_...  14.6 us
    select_n x1, other arithmetic, per_device(): outgoing = jnp.take(requests, source_req, axis=0)  14.1 us
    gather x1, local copies, waits for them, and re-layouts, per_device(): outgoing = jnp.take(requests, source_req, axis=0)  10.4 us
    gather x1, local copies, waits for them, and re-layouts, per_device(): jnp.take(adapter_down_weights, received_adapter_index[:, 0], axis=0)  10.4 us
    dynamic_update_slice x2, local copies, waits for them, and re-layouts, ring_gather(): lax.dynamic_update_slice_in_dim(out, from_left, (place - turn) % size * r...  9.14 us
  transfers between devices with their start and end apart: 6, of which 4 were waited for; matrix products, arithmetic and copies ran while one was open for 14% of the time, Pallas kernels for 0%

profile of v1, /device:TPU:0, one launch (start us, length us, event | category | flops | bytes accessed | tf_op | source)
XLA Modules:
  0.0 340.9 jit_solution(1150056410798482083)
XLA Ops:
  0.0 0.8 and_select_fusion
  1.3 0.7 gather_fusion
  2.7 5.2 %all-to-all-start.1 = ((s32[8,2,1]{1,2,0:T(1,128)}), s32[8,2,1]{1,2,0:T(1,128)S(1)}, u32[]{:S(2)}, u32[]{:S(2)}) async-start(s32[8,2,1]{1,2,0:T(1,128)} %bitcast.4), calls=%async_computation.1 | async-start | bytes 8192 | tf_op jit(solution)/shard_map/all_to_all | solution.py:59
  7.8 4.6 %all-to-all-done.1 = s32[8,2,1]{1,2,0:T(1,128)S(1)} async-done(((s32[8,2,1]{1,2,0:T(1,128)}), s32[8,2,1]{1,2,0:T(1,128)S(1)}, u32[]{:S(2)}, u32[]{:S(2)}) %all-to-all-start.1) | async-done | bytes 96 | tf_op jit(solution)/shard_map/all_to_all | solution.py:59
  12.9 0.7 reduce.5
  13.7 10.4 %gather_fusion.3 = bf16[16,64,8192]{2,1,0:T(8,128)(2,1)} fusion(bf16[8,64,8192]{2,1,0:T(8,128)(2,1)} %bitcast.18, s32[1024]{0:T(1024)S(1)} %pad_clamp_fusion.4), kind=kCustom, calls=%fused_computation.clone | custom fusion | bytes 33554496 | tf_op jit(solution)/shard_map/jit(_take)/gather | solution.py:56
  24.1 14.1 %broadcast_select_fusion = bf16[16,64,8192]{2,1,0:T(8,128)(2,1)} fusion(bf16[16,64,8192]{2,1,0:T(8,128)(2,1)} %gather_fusion.3, pred[16]{0:T(512)(128)(4,1)S(1)} %compare_and_fusion.1), kind=kLoop, calls=%fused_computation.8 | loop fusion | flops 8388608 | bytes 33554448 | tf_op jit(solution)/shard_map/jit(_take)/select_n | solution.py:56
  38.3 5.7 %all-to-all-start = ((bf16[16,64,8192]{2,1,0:T(8,128)(2,1)}), bf16[16,64,8192]{2,1,0:T(8,128)(2,1)}, u32[]{:S(2)}, u32[]{:S(2)}) async-start(bf16[16,64,8192]{2,1,0:T(8,128)(2,1)} %broadcast_select_fusion), calls=%async_computation | async-start | bytes 33554432 | tf_op jit(solution)/shard_map/all_to_all | solution.py:58
  44.0 1.6 collective-permute-start
  45.6 2.2 collective-permute-start.1
  48.0 0.7 gather_fusion.1
  48.7 90.9 %collective-permute-done = bf16[2048,1024]{1,0:T(8,128)(2,1)} collective-permute-done((bf16[2048,1024]{1,0:T(8,128)(2,1)}, bf16[2048,1024]{1,0:T(8,128)(2,1)}, u32[]{:S(2)}, u32[]{:S(2)}) %collective-permute-start) | collective-permute-done | bytes 4194336 | tf_op jit(solution)/shard_map/ppermute | solution.py:19
  139.6 10.4 %gather_fusion.4 = bf16[16,64,8192]{2,1,0:T(8,128)(2,1)} fusion(bf16[8,64,8192]{2,1,0:T(8,128)(2,1)} %param.9, s32[1024]{0:T(1024)S(1)} %pad_clamp_fusion.2), kind=kCustom, calls=%fused_computation.1.clone | custom fusion | bytes 33554496 | tf_op jit(solution)/shard_map/jit(_take)/gather | solution.py:61
  150.0 77.9 %all-to-all-done = bf16[16,64,8192]{2,1,0:T(8,128)(2,1)} async-done(((bf16[16,64,8192]{2,1,0:T(8,128)(2,1)}), bf16[16,64,8192]{2,1,0:T(8,128)(2,1)}, u32[]{:S(2)}, u32[]{:S(2)}) %all-to-all-start) | async-done | bytes 16777248 | tf_op jit(solution)/shard_map/all_to_all | solution.py:58
  228.0 14.6 %fusion.8 = bf16[16,64,1024]{2,1,0:T(8,128)(2,1)} fusion(bf16[16,64,1024]{2,1,0:T(8,128)(2,1)S(1)} %gather_fusion.1, pred[16]{0:T(512)(128)(4,1)S(1)} %compare_and_fusion, bf16[16,64,8192]{2,1,0:T(8,128)(2,1)} %all-to-all-done, bf16[16,64,8192]{2,1,0:T(8,128)(2,1)} %gather_fusion.4), kind=kOutput, calls=%fused_computation.15 | convolution fusion | flops 1218510848 | bytes 37748752 | tf_op jit(solution)/shard_map/sqr,srk->sqk/dot_general | solution.py:66
  242.6 3.8 %all-to-all-start.2 = ((bf16[16,64,1024]{2,1,0:T(8,128)(2,1)}), bf16[16,64,1024]{2,1,0:T(8,128)(2,1)S(1)}, u32[]{:S(2)}, u32[]{:S(2)}) async-start(bf16[16,64,1024]{2,1,0:T(8,128)(2,1)} %fusion.8), calls=%async_computation.2 | async-start | bytes 4194304 | tf_op jit(solution)/shard_map/all_to_all | solution.py:69
  246.6 6.6 %broadcast_in_dim.70 = bf16[8192,1024]{1,0:T(8,128)(2,1)} broadcast(bf16[]{:T(256)} %constant.100.clone.1), dimensions={} | broadcast | bytes 16777218 | tf_op jit(solution)/shard_map/broadcast_in_dim | solution.py:14
  253.2 2.4 constant_dynamic-update-slice_fusion.3
  255.6 4.6 %constant_dynamic-update-slice_fusion.2 = bf16[8192,1024]{1,0:T(8,128)(2,1)} fusion(bf16[8192,1024]{1,0:T(8,128)(2,1)} %constant_dynamic-update-slice_fusion.3, bf16[2048,1024]{1,0:T(8,128)(2,1)} %collective-permute-done, s32[]{:T(128)S(6)} %select_n.130), kind=kLoop, calls=%fused_computation.43 | loop fusion | bytes 8388612 | tf_op jit(solution)/shard_map/dynamic_update_slice | solution.py:20
  260.2 4.6 %constant_dynamic-update-slice_fusion.1 = bf16[8192,1024]{1,0:T(8,128)(2,1)} fusion(bf16[8192,1024]{1,0:T(8,128)(2,1)} %constant_dynamic-update-slice_fusion.2, bf16[2048,1024]{1,0:T(8,128)(2,1)} %collective-permute-done.1, s32[]{:T(128)S(6)} %select_n.132), kind=kLoop, calls=%fused_computation.42 | loop fusion | bytes 8388612 | tf_op jit(solution)/shard_map/dynamic_update_slice | solution.py:25
  264.8 54.1 %collective-permute-done.2 = bf16[2048,1024]{1,0:T(8,128)(2,1)} collective-permute-done((bf16[2048,1024]{1,0:T(8,128)(2,1)}, bf16[2048,1024]{1,0:T(8,128)(2,1)}, u32[]{:S(2)}, u32[]{:S(2)}) %collective-permute-start.2) | collective-permute-done | bytes 4194336 | tf_op jit(solution)/shard_map/ppermute | solution.py:19
  318.8 4.6 %constant_dynamic-update-slice_fusion = bf16[8192,1024]{1,0:T(8,128)(2,1)} fusion(bf16[8192,1024]{1,0:T(8,128)(2,1)} %constant_dynamic-update-slice_fusion.1, bf16[2048,1024]{1,0:T(8,128)(2,1)} %collective-permute-done.2, s32[]{:T(128)S(6)} %select_n.134), kind=kLoop, calls=%fused_computation.41 | loop fusion | bytes 8388612 | tf_op jit(solution)/shard_map/dynamic_update_slice | solution.py:20
  324.6 15.0 %fusion.4 = bf16[512,1024]{0,1:T(8,128)(2,1)S(1)} fusion(bf16[8192,1024]{1,0:T(8,128)(2,1)} %constant_dynamic-update-slice_fusion, bf16[512,8192]{1,0:T(8,128)(2,1)} %param.7, bf16[512,1024]{0,1:T(8,128)(2,1)S(1)} %copy.14, pred[512]{0:T(512)(128)(4,1)S(1)} %broadcast_in_dim.74), kind=kOutput, calls=%fused_computation.11 | convolution fusion | flops 8592031744 | bytes 27263488 | tf_op jit(solution)/shard_map/dot_general | solution.py:41
  339.6 1.3 copy.15
  (35 shorter events, 3.3 us)
Async XLA Ops:
  0.0 48.0 %copy-start = (bf16[8,64,1024]{2,1,0:T(8,128)(2,1)S(1)}, bf16[8,64,1024]{2,1,0:T(8,128)(2,1)}, u32[]{:S(2)}) copy-start(bf16[8,64,1024]{2,1,0:T(8,128)(2,1)} %param.10) | copy-start | bytes 3145732
  2.7 9.8 %all-to-all-start.1 = ((s32[8,2,1]{1,2,0:T(1,128)}), s32[8,2,1]{1,2,0:T(1,128)S(1)}, u32[]{:S(2)}, u32[]{:S(2)}) async-start(s32[8,2,1]{1,2,0:T(1,128)} %bitcast.4), calls=%async_computation.1 | async-start | bytes 8192 | tf_op jit(solution)/shard_map/all_to_all | solution.py:59
  38.3 189.7 %all-to-all-start = ((bf16[16,64,8192]{2,1,0:T(8,128)(2,1)}), bf16[16,64,8192]{2,1,0:T(8,128)(2,1)}, u32[]{:S(2)}, u32[]{:S(2)}) async-start(bf16[16,64,8192]{2,1,0:T(8,128)(2,1)} %broadcast_select_fusion), calls=%async_computation | async-start | bytes 33554432 | tf_op jit(solution)/shard_map/all_to_all | solution.py:58
  44.0 95.6 %collective-permute-start = (bf16[2048,1024]{1,0:T(8,128)(2,1)}, bf16[2048,1024]{1,0:T(8,128)(2,1)}, u32[]{:S(2)}, u32[]{:S(2)}) collective-permute-start(bf16[2048,1024]{1,0:T(8,128)(2,1)} %param.8), channel_id=1, source_target_pairs={{0,1},{1,2},{2,3},{3,0},{4,5},{5,6},{6,7},{7,4},{8,9},{9,10},{10,1... | collective-permute-start | bytes 12582920 | tf_op jit(solution)/shard_map/ppermute | solution.py:19
  45.6 214.5 %collective-permute-start.1 = (bf16[2048,1024]{1,0:T(8,128)(2,1)}, bf16[2048,1024]{1,0:T(8,128)(2,1)}, u32[]{:S(2)}, u32[]{:S(2)}) collective-permute-start(bf16[2048,1024]{1,0:T(8,128)(2,1)} %param.8), channel_id=1, source_target_pairs={{0,3},{1,0},{2,1},{3,2},{4,7},{5,4},{6,5},{7,6},{8,11},{9,8},{10,9... | collective-permute-start | bytes 12582920 | tf_op jit(solution)/shard_map/ppermute | solution.py:24
  139.6 179.2 %collective-permute-start.2 = (bf16[2048,1024]{1,0:T(8,128)(2,1)}, bf16[2048,1024]{1,0:T(8,128)(2,1)}, u32[]{:S(2)}, u32[]{:S(2)}) collective-permute-start(bf16[2048,1024]{1,0:T(8,128)(2,1)} %collective-permute-done), channel_id=1, source_target_pairs={{0,1},{1,2},{2,3},{3,0},{4,5},{5,6},{6,7},{7,4},{8,9},{9,10},{10,1... | collective-permute-start | bytes 12582920 | tf_op jit(solution)/shard_map/ppermute | solution.py:19
  242.6 80.9 %all-to-all-start.2 = ((bf16[16,64,1024]{2,1,0:T(8,128)(2,1)}), bf16[16,64,1024]{2,1,0:T(8,128)(2,1)S(1)}, u32[]{:S(2)}, u32[]{:S(2)}) async-start(bf16[16,64,1024]{2,1,0:T(8,128)(2,1)} %fusion.8), calls=%async_computation.2 | async-start | bytes 4194304 | tf_op jit(solution)/shard_map/all_to_all | solution.py:69
  246.6 6.6 %copy-start.2 = (bf16[2048,1024]{1,0:T(8,128)(2,1)S(1)}, bf16[2048,1024]{1,0:T(8,128)(2,1)}, u32[]{:S(2)}) copy-start(bf16[2048,1024]{1,0:T(8,128)(2,1)} %param.8) | copy-start | bytes 12582916
  324.6 16.3 %copy-start.1 = (bf16[8,64,1024]{2,1,0:T(8,128)(2,1)S(1)}, bf16[8,64,1024]{2,1,0:T(8,128)(2,1)}, u32[]{:S(2)}) copy-start(bf16[8,64,1024]{2,1,0:T(8,128)(2,1)} %param.10) | copy-start | bytes 3145732
